TPU v7x, 32 devices: a whole 2x2x4 slice. The times are simulated.
32 devices in a mesh: groups: 1, wide: 8 (over z, core), narrow: 4 (over y, x).
Axes of the slice: x: 2, y: 2, z: 4, core: 2. Of those that a mesh axis runs over, the one named last changes fastest.
Arguments:
- tokens: bfloat16 [256, 8192], P(('groups', 'narrow'), 'wide'), may hold values from -6 to 6
- norm_gain: bfloat16 [8192], P('wide'), may hold values from 0.099609375 to 1.8984375
- gate_blocks: bfloat16 [256, 80, 4096], P(('wide', 'narrow')), may hold values from -0.09375 to 0.09375
- gate_ids: int32 [256, 80], P(('wide', 'narrow')), may hold values from -1 to 127, as said below
- up_blocks: bfloat16 [256, 80, 4096], P(('wide', 'narrow')), may hold values from -0.09375 to 0.09375
- up_ids: int32 [256, 80], P(('wide', 'narrow')), may hold values from -1 to 127, as said below
- down_blocks: bfloat16 [256, 80, 4096], P(('wide', 'narrow')), may hold values from -0.0625 to 0.0625
- down_ids: int32 [256, 80], P(('wide', 'narrow')), may hold values from -1 to 127, as said below
Outputs:
- layer_output: bfloat16 [256, 8192], P(('groups', 'narrow'), 'wide')
Inputs may be any that keep to these rules, and one draw needn't show every extreme that they name: `gate_ids`: each row lists distinct width blocks in its first slots and -1 in the rest; every row lists between 48 and 80 blocks, and some row lists exactly 80. `up_ids`: as for gate_ids. `down_ids`: as for gate_ids.
All inputs are finite; a program needn't handle non-finite values.
Results may differ from a plain program's by a relative error of at most 0.0064.
Values may be sent and summed in bfloat16 or wider, within the bound.
A program may use at most 256 MiB of HBM per device.

v0:
```python
import jax
import jax.numpy as jnp
from jax import lax
from jax.sharding import PartitionSpec as P

BLOCK = 64


def normalize(gathered, gain_all):
    values = gathered.astype(jnp.float32)
    inverse_rms = lax.rsqrt(jnp.mean(values * values, axis=-1, keepdims=True) + 1e-05)
    return (values * inverse_rms * gain_all.astype(jnp.float32)).astype(jnp.bfloat16)


def project_in(normed, part, block_list):
    row_count, width_total = normed.shape
    count_blocks, slot_count = block_list.shape
    pieces = normed.reshape(row_count, width_total // BLOCK, BLOCK)
    picked = jnp.take(pieces, jnp.maximum(block_list, 0).reshape(-1), axis=1)
    picked = picked.reshape(row_count, count_blocks, slot_count, BLOCK)
    tiles = jnp.where((block_list >= 0)[:, :, None], part, jnp.zeros_like(part))
    tiles = tiles.reshape(count_blocks, slot_count, BLOCK, BLOCK)
    result = jnp.einsum("rfkc,fkcj->rfj", picked, tiles, preferred_element_type=jnp.float32)
    return result.reshape(row_count, count_blocks * BLOCK)


def dense_down(part, block_list, width_total):
    count_blocks, slot_count = block_list.shape
    width_blocks = width_total // BLOCK
    selector = jax.nn.one_hot(block_list, width_blocks, dtype=jnp.bfloat16)
    tiles = part.reshape(count_blocks, slot_count, BLOCK, BLOCK)
    placed = jnp.einsum("fkb,fkij->fibj", selector, tiles, preferred_element_type=jnp.bfloat16)
    return placed.reshape(count_blocks * BLOCK, width_total)


def gated_hidden(normed, gate_part, gate_list, up_part, up_list):
    gate_value = project_in(normed, gate_part, gate_list)
    upward = project_in(normed, up_part, up_list)
    return (jax.nn.silu(gate_value) * upward).astype(jnp.bfloat16)


def local(tokens, norm_gain, gate_blocks, gate_ids, up_blocks, up_ids, down_blocks, down_ids):
    gathered, gain_all = (
        lax.all_gather(tokens, "wide", axis=1, tiled=True),
        lax.all_gather(norm_gain, "wide", axis=0, tiled=True),
    )
    normed = normalize(gathered, gain_all)
    group_normed = lax.all_gather(normed, "narrow", axis=0, tiled=True)
    local_hidden = gated_hidden(group_normed, gate_blocks, gate_ids, up_blocks, up_ids)
    hidden = lax.all_to_all(local_hidden, "narrow", split_axis=0, concat_axis=1, tiled=True)
    down_all, down_list = (
        lax.all_gather(down_blocks, "narrow", axis=0, tiled=True),
        lax.all_gather(down_ids, "narrow", axis=0, tiled=True),
    )
    panel_dense = dense_down(down_all, down_list, gathered.shape[1])
    partial_value = jnp.dot(hidden, panel_dense, preferred_element_type=jnp.float32)
    return lax.psum_scatter(partial_value, "wide", scatter_dimension=1, tiled=True).astype(
        jnp.bfloat16
    )


def solution(mesh):
    placed = (
        P(("groups", "narrow"), "wide"),
        P("wide"),
        P(("wide", "narrow"), None, None),
        P(("wide", "narrow"), None),
        P(("wide", "narrow"), None, None),
        P(("wide", "narrow"), None),
        P(("wide", "narrow"), None, None),
        P(("wide", "narrow"), None),
    )
    return jax.shard_map(
        local,
        mesh=mesh,
        in_specs=placed,
        out_specs=P(("groups", "narrow"), "wide"),
        check_vma=False,
    )
```

profile of v0, /device:TPU:0, one launch (start us, length us, event | category | flops | bytes accessed | tf_op | source)
XLA Modules:
  0.0 514.7 jit_solution(6858604142762896944)
XLA Ops:
  7.3 14.5 %all_gather.16 = bf16[8192]{0:T(1024)(128)(2,1)S(1)} all-gather(bf16[1024]{0:T(1024)(128)(2,1)} %param.11), channel_id=1, replica_groups=mesh['groups'=1,'wide'=8,'narrow'=4] {'wide'}, dimensions={0}, use_global_device_ids=true | all-gather | bytes 18432 | tf_op jit(solution)/shard_map/all_gather | solution.py:45
  21.8 12.0 %all-gather.4.cloned.1.call-done = bf16[64,8192]{1,0:T(8,128)(2,1)} async-done(((bf16[64,1024]{1,0:T(8,128)(2,1)}), bf16[64,8192]{1,0:T(8,128)(2,1)}) %all-gather.4.cloned.1.call-update) | async-done | bytes 1048592 | tf_op jit(solution)/shard_map/all_gather | solution.py:44
  35.3 2.5 fusion.2
  40.8 5.2 %broadcast_select_fusion.3 = bf16[8,80,4096]{2,1,0:T(8,128)(2,1)} fusion(bf16[8,80,4096]{2,1,0:T(8,128)(2,1)} %param.12, pred[8,80]{1,0:T(8,128)(4,1)S(1)} %broadcast_compare_fusion.1), kind=kLoop, calls=%fused_computation.5 | loop fusion | flops 2621440 | bytes 10486400 | tf_op jit(solution)/shard_map/jit(_where)/select_n | solution.py:21
  46.1 15.3 %reshape.56 = bf16[8,80,64,64]{3,2,1,0:T(8,128)(2,1)} reshape(bf16[8,80,4096]{2,1,0:T(8,128)(2,1)} %broadcast_select_fusion.3) | data formatting | bytes 10485760 | tf_op jit(solution)/shard_map/reshape | solution.py:22
  61.4 5.4 %broadcast_select_fusion.2 = bf16[8,80,4096]{2,1,0:T(8,128)(2,1)} fusion(bf16[8,80,4096]{2,1,0:T(8,128)(2,1)} %param.14, pred[8,80]{1,0:T(8,128)(4,1)S(1)} %broadcast_compare_fusion), kind=kLoop, calls=%fused_computation.4 | loop fusion | flops 2621440 | bytes 10486400 | tf_op jit(solution)/shard_map/jit(_where)/select_n | solution.py:21
  66.8 15.2 %reshape.61 = bf16[8,80,64,64]{3,2,1,0:T(8,128)(2,1)} reshape(bf16[8,80,4096]{2,1,0:T(8,128)(2,1)} %broadcast_select_fusion.2) | data formatting | bytes 10485760 | tf_op jit(solution)/shard_map/reshape | solution.py:22
  82.0 8.3 %all-gather.6.cloned.1.call-done = bf16[256,8192]{1,0:T(8,128)(2,1)} async-done(((bf16[64,8192]{1,0:T(8,128)(2,1)}), bf16[256,8192]{1,0:T(8,128)(2,1)}) %all-gather.6.cloned.1.call-update) | async-done | bytes 4194320 | tf_op jit(solution)/shard_map/all_gather | solution.py:48
  90.4 6.4 %copy.22 = bf16[256,8192]{0,1:T(8,128)(2,1)} copy(bf16[256,8192]{1,0:T(8,128)(2,1)} %all-gather.6.cloned.1.call-done) | data formatting | bytes 8388608 | tf_op jit(solution)/shard_map/all_gather | solution.py:48
  96.8 19.0 %gather_fusion.1 = bf16[640,256,64]{1,2,0:T(8,128)(2,1)} fusion(bf16[256,128,64]{0,2,1:T(8,128)(2,1)} %bitcast.39, s32[1024]{0:T(1024)S(1)} %pad_clamp_fusion), kind=kCustom, calls=%fused_computation.1.clone | custom fusion | bytes 41945600 | tf_op jit(solution)/shard_map/jit(_take)/gather | solution.py:19
  115.8 18.0 %broadcast_select_fusion = bf16[640,256,64]{1,2,0:T(8,128)(2,1)} fusion(bf16[640,256,64]{1,2,0:T(8,128)(2,1)} %gather_fusion.1, pred[640]{0:T(1024)(128)(4,1)S(1)} %compare_and_fusion), kind=kLoop, calls=%fused_computation.2 | loop fusion | flops 10485760 | bytes 41943680 | tf_op jit(solution)/shard_map/jit(_take)/select_n | solution.py:19
  133.8 12.0 %convolution_bitcast_fusion = f32[256,8,64]{0,2,1:T(8,128)S(1)} fusion(bf16[8,80,64,64]{3,2,1,0:T(8,128)(2,1)} %reshape.61, bf16[256,8,80,64]{0,3,2,1:T(8,128)(2,1)} %bitcast.42), kind=kOutput, calls=%fused_computation.13 | convolution fusion | flops 1342177280 | bytes 26738688 | tf_op jit(solution)/shard_map/rfkc,fkcj->rfj/dot_general | solution.py:23
  146.7 18.7 %gather_fusion = bf16[640,256,64]{1,2,0:T(8,128)(2,1)} fusion(bf16[256,128,64]{0,2,1:T(8,128)(2,1)} %bitcast.40, s32[1024]{0:T(1024)S(1)} %pad_clamp_fusion.1), kind=kCustom, calls=%fused_computation.clone | custom fusion | bytes 41945600 | tf_op jit(solution)/shard_map/jit(_take)/gather | solution.py:19
  165.4 18.5 %broadcast_select_fusion.1 = bf16[640,256,64]{1,2,0:T(8,128)(2,1)} fusion(bf16[640,256,64]{1,2,0:T(8,128)(2,1)} %gather_fusion, pred[640]{0:T(1024)(128)(4,1)S(1)} %compare_and_fusion.1), kind=kLoop, calls=%fused_computation.3 | loop fusion | flops 10485760 | bytes 41943680 | tf_op jit(solution)/shard_map/jit(_take)/select_n | solution.py:19
  183.9 12.0 %convolution_bitcast_fusion.1 = f32[256,8,64]{0,2,1:T(8,128)S(1)} fusion(bf16[8,80,64,64]{3,2,1,0:T(8,128)(2,1)} %reshape.56, bf16[256,8,80,64]{0,3,2,1:T(8,128)(2,1)} %bitcast.43), kind=kOutput, calls=%fused_computation.14 | convolution fusion | flops 1342177280 | bytes 26738688 | tf_op jit(solution)/shard_map/rfkc,fkcj->rfj/dot_general | solution.py:23
  197.6 3.4 all-to-all-start
  201.1 10.5 %all_gather.18 = s32[32,80]{1,0:T(8,128)S(1)} all-gather(s32[8,80]{1,0:T(8,128)S(1)} %copy-done.1), channel_id=1, replica_groups=mesh['groups'=1,'wide'=8,'narrow'=4] {'narrow'}, dimensions={0}, use_global_device_ids=true | all-gather | bytes 12800 | tf_op jit(solution)/shard_map/all_gather | solution.py:53
  211.6 76.8 %all-gather.8.cloned.1.call-done = bf16[32,80,4096]{2,1,0:T(8,128)(2,1)} async-done(((bf16[8,80,4096]{2,1,0:T(8,128)(2,1)}), bf16[32,80,4096]{2,1,0:T(8,128)(2,1)}) %all-gather.8.cloned.1.call-update) | async-done | bytes 20971536 | tf_op jit(solution)/shard_map/all_gather | solution.py:52
  288.4 21.6 %fusion.3 = bf16[32,128,4096]{1,2,0} fusion(bf16[32,80,4096]{2,1,0:T(8,128)(2,1)} %all-gather.8.cloned.1.call-done, s32[32,80]{1,0:T(8,128)S(1)} %all_gather.18), kind=kOutput, calls=%fused_computation.12 | convolution fusion | flops 2684682240 | bytes 54536192
  310.0 59.1 %copy.29 = bf16[32,64,128,64]{3,2,1,0:T(8,128)(2,1)} copy(bf16[32,64,128,64]{2,3,1,0:T(8,128)(2,1)} %bitcast.41) | data formatting | bytes 67108864 | tf_op jit(solution)/shard_map/fkb,fkij->fibj/transpose | solution.py:32
  369.1 86.6 %reshape.66 = bf16[2048,8192]{1,0:T(8,128)(2,1)} reshape(bf16[32,64,128,64]{3,2,1,0:T(8,128)(2,1)} %copy.29) | data formatting | bytes 67108864 | tf_op jit(solution)/shard_map/reshape | solution.py:33
  455.7 14.9 %fusion.5 = f32[64,8192]{1,0:T(8,128)} fusion(bf16[64,2048]{1,0:T(8,128)(2,1)S(1)} %bitcast.44, bf16[2048,8192]{1,0:T(8,128)(2,1)} %reshape.66), kind=kOutput, calls=%fused_computation.28 | convolution fusion | flops 2147483648 | bytes 35913728 | tf_op jit(solution)/shard_map/dot_general | solution.py:56
  470.6 36.0 %reduce-scatter.2.cloned.1.call-done = f32[64,1024]{1,0:T(8,128)} async-done(((f32[64,8192]{1,0:T(8,128)}), f32[64,1024]{1,0:T(8,128)}) %reduce-scatter.2.cloned.1.call-update) | async-done | bytes 262160 | tf_op jit(solution)/shard_map/reduce_scatter | solution.py:57
  506.6 1.6 convert_element_type.22
  (34 shorter events, 7.8 us)
Async XLA Ops:
  6.5 27.3 %all-gather.4.cloned.1.call-start = ((), (), s32[]{:S(2)}) async-start(), calls=%async_computation.2 | async-start | bytes 1179648 | tf_op jit(solution)/shard_map/all_gather | solution.py:44
  7.3 83.1 %all-gather.6.cloned.1.call-start = ((), (), s32[]{:S(2)}) async-start(), calls=%async_computation.3 | async-start | bytes 5242880 | tf_op jit(solution)/shard_map/all_gather | solution.py:48
  37.9 250.6 %all-gather.8.cloned.1.call-start = ((), (), s32[]{:S(2)}) async-start(), calls=%async_computation.4 | async-start | bytes 26214400 | tf_op jit(solution)/shard_map/all_gather | solution.py:52
  46.1 15.3 %copy-start = (s32[8,80]{1,0:T(8,128)S(1)}, s32[8,80]{1,0:T(8,128)}, u32[]{:S(2)}) copy-start(s32[8,80]{1,0:T(8,128)} %param.15) | copy-start | bytes 7684
  183.9 17.2 %copy-start.1 = (s32[8,80]{1,0:T(8,128)S(1)}, s32[8,80]{1,0:T(8,128)}, u32[]{:S(2)}) copy-start(s32[8,80]{1,0:T(8,128)} %param.17) | copy-start | bytes 7684
  197.6 14.0 %all-to-all-start = ((bf16[4,64,512]{2,1,0:T(8,128)(2,1)}), bf16[4,64,512]{2,1,0:T(8,128)(2,1)S(1)}, u32[]{:S(2)}, u32[]{:S(2)}) async-start(bf16[4,64,512]{2,1,0:T(8,128)(2,1)} %multiply_convert_fusion), calls=%async_computation | async-start | bytes 524288 | tf_op jit(solution)/shard_map/all_to_all | solution.py:50
  201.0 305.5 %reduce-scatter.2.cloned.1.call-start = ((), (), s32[]{:S(2)}) async-start(), calls=%async_computation.5 | async-start | bytes 2359296 | tf_op jit(solution)/shard_map/reduce_scatter | solution.py:57
Sparse Core Ops, SparseCore 0:
  9.0 24.7 all-gather.3
  38.0 52.3 all-gather.5
  92.2 196.1 all-gather.7
  470.7 35.7 reduce-scatter.1
where the time goes:
time: 520 us; the launch traced here: 515 us
  local copies, waits for them, and re-layouts  222 us (43%)
  waiting for transfers between devices  135 us (26%)
  matrix products  60.5 us (12%)
  other arithmetic  55.8 us (11%)
  blocking collectives  25 us (5%)
  between operations  13.2 us (3%)
    reshape x1, local copies, waits for them, and re-layouts, dense_down(): return placed.reshape(count_blocks * BLOCK, width_total)  86.6 us
    all_gather x1, waiting for transfers between devices, local(): lax.all_gather(down_blocks, 'narrow', axis=0, tiled=True)  76.8 us
    transpose x1, local copies, waits for them, and re-layouts, dense_down(): jnp.einsum('fkb,fkij->fibj', selector, tiles, preferred_element_type=jnp....  59.1 us
    gather x2, local copies, waits for them, and re-layouts, project_in(): picked = jnp.take(pieces, jnp.maximum(block_list, 0).reshape(-1), axis=1)  37.7 us
    select_n x4, other arithmetic, project_in(): picked = jnp.take(pieces, jnp.maximum(block_list, 0).reshape(-1), axis=1)  36.6 us
    reduce_scatter x1, waiting for transfers between devices, local(): lax.psum_scatter(partial_value, 'wide', scatter_dimension=1, tiled=True)  36 us
    reshape x2, local copies, waits for them, and re-layouts, project_in(): tiles = tiles.reshape(count_blocks, slot_count, BLOCK, BLOCK)  30.5 us
    dot_general x2, matrix products, project_in(): jnp.einsum('rfkc,fkcj->rfj', picked, tiles, preferred_element_type=jnp.fl...  24.1 us
  transfers between devices with their start and end apart: 5, of which 4 were waited for; matrix products, arithmetic and copies ran while one was open for 29% of the time, Pallas kernels for 0%

commit v1 on v0

--- a/solution.py
+++ b/solution.py
@@ -1,9 +1,15 @@
+import functools
+
 import jax
 import jax.numpy as jnp
 from jax import lax
+from jax.experimental import pallas as pl
+from jax.experimental.pallas import tpu as pltpu
 from jax.sharding import PartitionSpec as P
 
 BLOCK = 64
+BF = jnp.bfloat16
+F32 = jnp.float32
 
 
 def normalize(gathered, gain_all):
@@ -39,7 +45,7 @@
     return (jax.nn.silu(gate_value) * upward).astype(jnp.bfloat16)
 
 
-def local(tokens, norm_gain, gate_blocks, gate_ids, up_blocks, up_ids, down_blocks, down_ids):
+def plain(tokens, norm_gain, gate_blocks, gate_ids, up_blocks, up_ids, down_blocks, down_ids):
     gathered, gain_all = (
         lax.all_gather(tokens, "wide", axis=1, tiled=True),
         lax.all_gather(norm_gain, "wide", axis=0, tiled=True),
@@ -57,6 +63,177 @@
     return lax.psum_scatter(partial_value, "wide", scatter_dimension=1, tiled=True).astype(
         jnp.bfloat16
     )
+
+
+def one_hot(rows, columns, source_of):
+    r = lax.broadcasted_iota(jnp.int32, (rows, columns), 0)
+    d = lax.broadcasted_iota(jnp.int32, (rows, columns), 1)
+    return jnp.where(r == source_of(d), 1.0, 0.0).astype(BF)
+
+
+def low_half(rows):
+    return lax.broadcasted_iota(jnp.int32, (rows, 128), 1) < 64
+
+
+def swap(x):
+    return pltpu.roll(x, 64, 1)
+
+
+class Panels:
+    def __init__(self, blocks, ids, raw, sel, turn, in_w, down_w, sems):
+        self.blocks, self.ids, self.raw, self.sel, self.turn = blocks, ids, raw, sel, turn
+        self.in_w, self.down_w, self.sems = in_w, down_w, sems
+        self.pairs = blocks[0].shape[0] // 2
+        self.slots = blocks[0].shape[1]
+        self.steps = [(k, q) for k in range(3) for q in range(self.pairs)]
+
+    def copies(self, n):
+        kind, q = self.steps[n]
+        return [
+            pltpu.make_async_copy(
+                self.blocks[kind].at[2 * q + e],
+                self.raw.at[n % 2, pl.ds(128 * e, self.slots)],
+                self.sems.at[n % 2, e],
+            )
+            for e in range(2)
+        ]
+
+    def begin(self):
+        self.raw[...] = jnp.zeros_like(self.raw)
+        self.sel[...] = jnp.zeros_like(self.sel)
+        for c in self.copies(0):
+            c.start()
+
+    def step(self, n):
+        kind, q = self.steps[n]
+        if n + 1 < len(self.steps):
+            for c in self.copies(n + 1):
+                c.start()
+        row = lax.broadcasted_iota(jnp.int32, (128, self.slots), 0)
+        if kind == 2:
+            row = 2 * (row % 64) + row // 64
+        for e in range(2):
+            hit = self.ids[kind][2 * q + e : 2 * q + e + 1, :] == row
+            self.sel[128 * e : 128 * e + 128, 128 * e : 128 * e + self.slots] = jnp.where(hit, 1.0, 0.0).astype(BF)
+        for c in self.copies(n):
+            c.wait()
+        if kind < 2:
+            self.place_in(n % 2, (kind * self.pairs + q) * 128)
+        else:
+            self.place_down(n % 2, q)
+
+    def picked(self, slot, c):
+        lanes = pl.ds(pl.multiple_of(c * 256, 256), 256)
+        return jnp.dot(self.sel[...], self.raw[slot, :, lanes], preferred_element_type=F32)
+
+    def place_in(self, slot, column):
+        low = low_half(128)
+
+        def body(c, carry):
+            s = self.picked(slot, c)
+            for k in range(2):
+                a = s[:128, 128 * k : 128 * k + 128]
+                b = swap(s[128:, 128 * k : 128 * k + 128])
+                at = pl.ds(pl.multiple_of((2 * c + k) * 16, 16), 16)
+                for p, v in enumerate((jnp.where(low, a, b), jnp.where(low, b, a))):
+                    self.in_w[p, :, at, column : column + 128] = v.astype(BF).reshape(8, 16, 128)
+            return carry
+
+        lax.fori_loop(0, 16, body, 0)
+
+    def place_down(self, slot, q):
+        low = low_half(64)
+
+        def body(c, carry):
+            s = self.picked(slot, c)
+            for k in range(2):
+                for e in range(2):
+                    a = s[128 * e : 128 * e + 64, 128 * k : 128 * k + 128]
+                    b = s[128 * e + 64 : 128 * e + 128, 128 * k : 128 * k + 128]
+                    at = pl.ds(2 * c + k, 64, stride=32)
+                    self.turn[2 * e, at, :] = jnp.where(low, a, swap(b))
+                    self.turn[2 * e + 1, at, :] = jnp.where(low, swap(a), b)
+            return carry
+
+        lax.fori_loop(0, 16, body, 0)
+        for e in range(2):
+            for p in range(2):
+                first = p * 64 * self.pairs + (2 * q + e) * 32
+                for b in range(64):
+                    self.down_w[first : first + 32, 128 * b : 128 * b + 128] = self.turn[
+                        2 * e + p, 32 * b : 32 * b + 32, :
+                    ].astype(BF)
+
+
+def gather_product(x_ref, in_w, acc, w, first):
+    for p in range(2):
+        term = jnp.dot(x_ref[w, :, 512 * p : 512 * p + 512], in_w[p, w], preferred_element_type=F32)
+        if first:
+            acc[p] = term
+        else:
+            acc[p] += term
+
+
+def hidden_of(acc, half):
+    cols = []
+    for t in range(2 * half // 128):
+        at = slice(128 * t, 128 * t + 128)
+        cols.append(acc[0, :, at] + swap(acc[1, :, at]))
+    count = half // 128
+    out = [(jax.nn.silu(cols[t]) * cols[count + t]).astype(BF) for t in range(count)]
+    h = jnp.concatenate(out, axis=1)
+    quarter = half // 2
+
+    def source(d):
+        return (d % quarter) // 32 * 64 + 2 * (d % 32) + d // quarter
+
+    return jnp.dot(h, one_hot(half, half, source), preferred_element_type=F32).astype(BF)
+
+
+def compute_kernel(x_ref, gi, ui, di, gb, ub, db, out, raw, sel, turn, in_w, down_w, acc, sems):
+    panels = Panels((gb, ub, db), (gi, ui, di), raw, sel, turn, in_w, down_w, sems)
+    panels.begin()
+    for n in range(len(panels.steps)):
+        panels.step(n)
+    for w in range(8):
+        gather_product(x_ref, in_w, acc, w, w == 0)
+    h = hidden_of(acc, in_w.shape[3] // 2)
+    for w in range(8):
+        out[w] = jnp.dot(h, down_w[:, 1024 * w : 1024 * w + 1024], preferred_element_type=F32)
+
+
+def compute(x, gate_ids, up_ids, down_ids, gate_blocks, up_blocks, down_blocks):
+    count = gate_blocks.shape[0]
+    rows = x.shape[1]
+    vmem = pl.BlockSpec(memory_space=pltpu.VMEM)
+    return pl.pallas_call(
+        compute_kernel,
+        out_shape=jax.ShapeDtypeStruct(x.shape, F32),
+        in_specs=[vmem] * 4 + [pl.BlockSpec(memory_space=pl.ANY)] * 3,
+        out_specs=vmem,
+        scratch_shapes=[
+            pltpu.VMEM((2, 256, 4096), BF),
+            pltpu.VMEM((256, 256), BF),
+            pltpu.VMEM((4, 2048, 128), F32),
+            pltpu.VMEM((2, 8, 512, 128 * count), BF),
+            pltpu.VMEM((64 * count, 8192), BF),
+            pltpu.VMEM((2, rows, 128 * count), F32),
+            pltpu.SemaphoreType.DMA((2, 2)),
+        ],
+        compiler_params=pltpu.CompilerParams(vmem_limit_bytes=60 * 1024 * 1024),
+    )(x, gate_ids, up_ids, down_ids, gate_blocks, up_blocks, down_blocks)
+
+
+def fused(tokens, norm_gain, gate_blocks, gate_ids, up_blocks, up_ids, down_blocks, down_ids):
+    rows, width = tokens.shape
+    values = tokens.astype(F32)
+    total = lax.psum(jnp.sum(values * values, axis=-1, keepdims=True), "wide")
+    normed = (values * lax.rsqrt(total / 8192.0 + 1e-05) * norm_gain.astype(F32)).astype(BF)
+    turned = normed.reshape(rows, width // 64, 32, 2).transpose(0, 3, 2, 1).reshape(rows, width)
+    x = lax.all_gather(turned, ("wide", "narrow"), axis=0, tiled=False).reshape(8, 4 * rows, width)
+    part = compute(x, gate_ids, up_ids, down_ids, gate_blocks, up_blocks, down_blocks)
+    part = part.reshape(32 * rows, width)
+    return lax.psum_scatter(part, ("wide", "narrow"), scatter_dimension=0, tiled=True).astype(BF)
 
 
 def solution(mesh):
@@ -70,6 +247,7 @@
         P(("wide", "narrow"), None, None),
         P(("wide", "narrow"), None),
     )
+    local = fused if mesh.shape["wide"] == 8 and mesh.shape["narrow"] == 4 else plain
     return jax.shard_map(
         local,
         mesh=mesh,

time: 520 us -> 360 us (0.69)
  local copies, waits for them, and re-layouts: 222 us -> 2.03 us
  waiting for transfers between devices: 135 us -> 243 us
  Pallas kernels: 0 us -> 81.1 us
  matrix products: 60.5 us -> 0 us
  other arithmetic: 55.8 us -> 2.67 us
  blocking collectives: 25 us -> 18.1 us
    reduce_scatter x1, waiting for transfers between devices: 36 us -> 182 us  [fused(): lax.psum_scatter(part, ('wide', 'narrow'), scatter_dimension=0, tiled=True)]
    reshape x9 -> x0, local copies, waits for them, and re-layouts: 119 us -> none  [the longest x1 86.6 us: dense_down(): return placed.reshape(count_blocks * BLOCK, width_total)]
    pallas_call x0 -> x1, Pallas kernels: none -> 81.1 us  [compute(): pl.pallas_call(compute_kernel, out_shape=jax.ShapeDtypeStruct(x.shape, F3...]
    transpose x1, local copies, waits for them, and re-layouts: 59.1 us -> 0.18 us  [fused(): normed.reshape(rows, width // 64, 32, 2).transpose(0, 3, 2, 1)]
    select_n x6 -> x0, other arithmetic: 47.2 us -> none  [the longest x4 36.6 us: project_in(): picked = jnp.take(pieces, jnp.maximum(block_list, 0).reshape(-1), axis=1)]
    dot_general x3 -> x0, matrix products: 39 us -> none  [the longest x2 24.1 us: project_in(): jnp.einsum('rfkc,fkcj->rfj', picked, tiles, preferred_element_type=jnp.fl...]
    gather x2 -> x0, local copies, waits for them, and re-layouts: 37.7 us -> none  [project_in(): picked = jnp.take(pieces, jnp.maximum(block_list, 0).reshape(-1), axis=1)]
    all_gather x3 -> x1, waiting for transfers between devices: 97.1 us -> 60.3 us  [fused(): lax.all_gather(turned, ('wide', 'narrow'), axis=0, tiled=False)]
  transfers between devices with their start and end apart: 5 -> 2, of which waited for: 4 -> 2; matrix products, arithmetic and copies ran while one was open for 29% -> 0% of each run, Pallas kernels for 0% -> 0%
where the time goes in v1:
time: 360 us
  waiting for transfers between devices  243 us (68%)
  Pallas kernels  81.1 us (23%)
  blocking collectives  18.1 us (5%)
  between operations  13.4 us (4%)
    reduce_scatter x1, waiting for transfers between devices, fused(): lax.psum_scatter(part, ('wide', 'narrow'), scatter_dimension=0, tiled=True)  182 us
    pallas_call x1, Pallas kernels, compute(): pl.pallas_call(compute_kernel, out_shape=jax.ShapeDtypeStruct(x.shape, F3...  81.1 us
    all_gather x1, waiting for transfers between devices, fused(): lax.all_gather(turned, ('wide', 'narrow'), axis=0, tiled=False)  60.3 us
    psum x1, blocking collectives, fused(): total = lax.psum(jnp.sum(values * values, axis=-1, keepdims=True), 'wide')  18.1 us
  transfers between devices with their start and end apart: 2, of which 2 were waited for; matrix products, arithmetic and copies ran while one was open for 0% of the time, Pallas kernels for 0%

profile of v1, /device:TPU:0, one launch (start us, length us, event | category | flops | bytes accessed | tf_op | source)
XLA Modules:
  0.0 359.9 jit_solution(1747408095271400205)
XLA Ops:
  6.5 0.0 all-gather.2.cloned.1.call-start
  6.5 0.7 convert_element_type.13
  7.2 1.1 copy.13
  8.3 0.2 fusion
  8.5 18.1 %psum.7 = f32[64,1]{0,1:T(1,128)S(1)} all-reduce(f32[64,1]{0,1:T(1,128)S(1)} %bitcast.13), channel_id=1, replica_groups=mesh['groups'=1,'wide'=8,'narrow'=4] {'wide'}, use_global_device_ids=true, to_apply=%region_1.0 | all-reduce | flops 64 | bytes 512 | tf_op jit(solution)/shard_map/psum | solution.py:230
  26.5 0.2 fusion.2
  26.7 0.2 copy.14
  26.9 0.8 copy.15
  27.7 0.0 all-gather.2.cloned.1.call-update
  27.7 0.0 reduce-scatter.2.cloned.1.call-start
  27.8 60.3 %all-gather.2.cloned.1.call-done = bf16[32,64,1024]{2,1,0:T(8,128)(2,1)} async-done(((bf16[1,64,1024]{2,1,0:T(8,128)(2,1)}), bf16[32,64,1024]{2,1,0:T(8,128)(2,1)}) %all-gather.2.cloned.1.call-update) | async-done | bytes 4194320 | tf_op jit(solution)/shard_map/all_gather | solution.py:233
  88.1 81.1 %shard_map.82 = f32[8,256,1024]{2,1,0:T(8,128)} custom-call(bf16[8,256,1024]{2,1,0:T(8,128)(2,1)} %bitcast.10, s32[8,80]{1,0:T(8,128)} %gi.1, s32[8,80]{1,0:T(8,128)} %ui.1, s32[8,80]{1,0:T(8,128)} %di.1, bf16[8,80,4096]{2,1,0:T(8,128)(2,1)} %gb.1, bf16[8,80,4096]{2,1,0:T(8,128)(2,1)} %ub.1, bf16[8,80,4096]{2,1,0:T(8,128)(2,1)} %db.1), custom_call_target="tpu_custom_call" | custom-call | tf_op jit(solution)/shard_map/pallas_call | solution.py:209
  169.2 0.0 reduce-scatter.2.cloned.1.call-update
  169.3 182.2 %reduce-scatter.2.cloned.1.call-done = f32[64,1024]{1,0:T(8,128)} async-done(((f32[2048,1024]{1,0:T(8,128)}), f32[64,1024]{1,0:T(8,128)}) %reduce-scatter.2.cloned.1.call-update) | async-done | bytes 262160 | tf_op jit(solution)/shard_map/reduce_scatter | solution.py:236
  351.5 1.6 convert_element_type.15
  (1 shorter events, 0.0 us)
Async XLA Ops:
  6.5 81.6 %all-gather.2.cloned.1.call-start = ((), (), s32[]{:S(2)}) async-start(), calls=%async_computation.1 | async-start | bytes 4325376 | tf_op jit(solution)/shard_map/all_gather | solution.py:233
  27.7 323.7 %reduce-scatter.2.cloned.1.call-start = ((), (), s32[]{:S(2)}) async-start(), calls=%async_computation.2 | async-start | bytes 8650752 | tf_op jit(solution)/shard_map/reduce_scatter | solution.py:236
Sparse Core Ops, SparseCore 0:
  27.9 60.2 all-gather.1
  169.4 182.0 reduce-scatter.1

commit v2 on v1

--- a/solution.py
+++ b/solution.py
@@ -190,26 +190,198 @@
     return jnp.dot(h, one_hot(half, half, source), preferred_element_type=F32).astype(BF)
 
 
-def compute_kernel(x_ref, gi, ui, di, gb, ub, db, out, raw, sel, turn, in_w, down_w, acc, sems):
+def fused_kernel(
+    tok, gain, gi, ui, di, gb, ub, db, out,
+    raw, sel, turn, in_w, down_w, acc, x, ssum, q, own, send0, land0, send1, land1, send2, land2, send3, land3,
+    sems, ss_s, ss_r, z_s, z_r, a_s, a_r, b_s, b_r, c_s, c_r, r0_s, r0_r, r1_s, r1_r, r2_s, r2_r, r3_s, r3_r,
+):
+    wide, narrow = lax.axis_index("wide"), lax.axis_index("narrow")
+    z, core = wide // 2, wide % 2
+    y, xx = narrow // 2, narrow % 2
+    sibling = {"wide": 2 * z + 1 - core}
+    beside = ({"narrow": 2 * y + 1 - xx}, {"narrow": 2 * (1 - y) + xx})
+    mine, other = (xx, y), (1 - xx, 1 - y)
+
+    def plane(d):
+        return (z + d) % 4
+
+    def rows(h, pair, half, count):
+        return pl.ds(pl.multiple_of(128 * h + 64 * pair + 32 * half, 32), count)
+
+    def remote(src, dst, s, r, to):
+        return pltpu.make_async_remote_copy(
+            src_ref=src, dst_ref=dst, send_sem=s, recv_sem=r, device_id=to, device_id_type=pl.DeviceIdType.MESH
+        )
+
+    def own_rows(h):
+        return rows(h, mine[1 - h], mine[h], 32)
+
+    values = tok[...].astype(F32)
+    ssum[0] = jnp.broadcast_to(jnp.sum(values * values, axis=-1, keepdims=True), ssum.shape[1:])
+
+    barrier = pltpu.get_barrier_semaphore()
+    peers = [{"wide": (wide + d) % 8} for d in range(1, 8)] + list(beside)
+    for peer in peers:
+        pl.semaphore_signal(barrier, inc=1, device_id=peer, device_id_type=pl.DeviceIdType.MESH)
+    pl.semaphore_wait(barrier, len(peers))
+
+    sums = [remote(ssum.at[0], ssum.at[d], ss_s.at[d], ss_r.at[d], peers[d - 1]) for d in range(1, 8)]
+    for c in sums:
+        c.start()
+
     panels = Panels((gb, ub, db), (gi, ui, di), raw, sel, turn, in_w, down_w, sems)
     panels.begin()
-    for n in range(len(panels.steps)):
+    panels.step(0)
+
+    total = jnp.sum(values * values, axis=-1, keepdims=True)
+    for d in range(1, 8):
+        sums[d - 1].wait_recv()
+        total = total + ssum[d, :, 0:1]
+    inverse = lax.rsqrt(total / 8192.0 + 1e-05)
+    normed = (values * inverse * gain[...].astype(F32)).astype(BF)
+    for t in range(8):
+
+        def source(d):
+            d = d + 128 * t
+            return (d % 16) * 64 + 2 * ((d % 512) // 16) + d // 512
+
+        part = jnp.dot(normed, one_hot(1024, 128, source), preferred_element_type=F32).astype(BF)
+        for h in range(2):
+            x[wide, own_rows(h), 128 * t : 128 * t + 128] = part[32 * h : 32 * h + 32]
+
+    def held(d):
+        return 2 * plane(4 - d) + core
+
+    along = {}
+    first = {}
+    second = {}
+    last = {}
+    for d in range(1, 4):
+        for h in range(2):
+            ref = x.at[wide, own_rows(h)]
+            along[d, h] = remote(ref, ref, z_s.at[d, h], z_r.at[d, h], {"wide": 2 * plane(d) + core})
+    for d in range(4):
+        for h in range(2):
+            ref = x.at[held(d), own_rows(h)]
+            first[d, h] = remote(ref, ref, a_s.at[d, h], a_r.at[d, h], beside[h])
+            ref = x.at[held(d), rows(h, mine[1 - h], 0, 64)]
+            second[d, h] = remote(ref, ref, b_s.at[d, h], b_r.at[d, h], beside[1 - h])
+        ref = x.at[held(d)]
+        last[d] = remote(ref, ref, c_s.at[d], c_r.at[d], sibling)
+
+    def go_first(d):
+        for h in range(2):
+            if d:
+                along[d, h].wait_recv()
+            first[d, h].start()
+
+    def go_second(d):
+        for h in range(2):
+            first[d, h].wait_recv()
+            second[d, h].start()
+
+    def go_last(d):
+        for h in range(2):
+            second[d, h].wait_recv()
+        last[d].start()
+
+    for c in along.values():
+        c.start()
+    go_first(0)
+    after = {
+        1: [(go_first, 1), (go_second, 0), (go_first, 2), (go_first, 3)],
+        2: [(go_second, 1), (go_last, 0)],
+        3: [(go_second, 2), (go_last, 1)],
+        4: [(go_second, 3), (go_last, 2)],
+        5: [(go_last, 3)],
+    }
+    for n in range(1, len(panels.steps)):
         panels.step(n)
-    for w in range(8):
-        gather_product(x_ref, in_w, acc, w, w == 0)
-    h = hidden_of(acc, in_w.shape[3] // 2)
-    for w in range(8):
-        out[w] = jnp.dot(h, down_w[:, 1024 * w : 1024 * w + 1024], preferred_element_type=F32)
-
-
-def compute(x, gate_ids, up_ids, down_ids, gate_blocks, up_blocks, down_blocks):
+        for act, d in after.get(n, ()):
+            act(d)
+
+    for d in range(4):
+        gather_product(x, in_w, acc, held(d), d == 0)
+    for d in range(4):
+        last[d].wait_recv()
+        gather_product(x, in_w, acc, held(d) + 1 - 2 * core, False)
+    hidden = hidden_of(acc, in_w.shape[3] // 2)
+
+    def product(w):
+        columns = pl.ds(pl.multiple_of(1024 * w, 1024), 1024)
+        return jnp.dot(hidden, down_w[:, columns], preferred_element_type=F32)
+
+    order = (1, 2, 3, 0)
+    hop0, hop1, hop2, hop3 = {}, {}, {}, {}
+    for e in order:
+        hop0[e] = remote(send0.at[e], land0.at[e], r0_s.at[e], r0_r.at[e], sibling)
+        for h in range(2):
+            hop1[e, h] = remote(send1.at[e, h], land1.at[e, h], r1_s.at[e, h], r1_r.at[e, h], beside[1 - h])
+            hop2[e, h] = remote(send2.at[e, h], land2.at[e, h], r2_s.at[e, h], r2_r.at[e, h], beside[h])
+        if e:
+            hop3[e] = remote(send3.at[e], land3.at[e], r3_s.at[e], r3_r.at[e], {"wide": 2 * plane(e) + core})
+    for e in order:
+        send0[e] = product(2 * plane(e) + 1 - core).astype(BF)
+        hop0[e].start()
+    for e in order:
+        q[e] = product(2 * plane(e) + core)
+
+    def go_hop1(e):
+        hop0[e].wait_recv()
+        for h in range(2):
+            at = rows(h, other[1 - h], 0, 64)
+            send1[e, h] = (q[e, at] + land0[e, at].astype(F32)).astype(BF)
+            hop1[e, h].start()
+        for h in range(2):
+            at = rows(h, mine[1 - h], 0, 64)
+            q[e, at] = q[e, at] + land0[e, at].astype(F32)
+
+    def go_hop2(e):
+        for h in range(2):
+            hop1[e, h].wait_recv()
+            at = rows(h, mine[1 - h], other[h], 32)
+            come = pl.ds(pl.multiple_of(32 * other[h], 32), 32)
+            send2[e, h] = (q[e, at] + land1[e, h, come].astype(F32)).astype(BF)
+            hop2[e, h].start()
+
+    def go_hop3(e):
+        for h in range(2):
+            hop2[e, h].wait_recv()
+            come = pl.ds(pl.multiple_of(32 * mine[h], 32), 32)
+            v = q[e, own_rows(h)] + land1[e, h, come].astype(F32) + land2[e, h].astype(F32)
+            if e:
+                send3[e, 32 * h : 32 * h + 32] = v.astype(BF)
+            else:
+                own[32 * h : 32 * h + 32] = v
+        if e:
+            hop3[e].start()
+
+    for k in range(6):
+        for lag, act in enumerate((go_hop1, go_hop2, go_hop3)):
+            if 0 <= k - lag < 4:
+                act(order[k - lag])
+    value = own[...]
+    for e in (1, 2, 3):
+        hop3[e].wait_recv()
+        value = value + land3[e].astype(F32)
+    out[...] = value.astype(BF)
+
+    for group in (along, first, second, last, hop0, hop1, hop2, hop3):
+        for c in group.values():
+            c.wait_send()
+    for c in sums:
+        c.wait_send()
+
+
+def fused(tokens, norm_gain, gate_blocks, gate_ids, up_blocks, up_ids, down_blocks, down_ids):
+    rows, width = tokens.shape
     count = gate_blocks.shape[0]
-    rows = x.shape[1]
     vmem = pl.BlockSpec(memory_space=pltpu.VMEM)
+    dma = pltpu.SemaphoreType.DMA
     return pl.pallas_call(
-        compute_kernel,
-        out_shape=jax.ShapeDtypeStruct(x.shape, F32),
-        in_specs=[vmem] * 4 + [pl.BlockSpec(memory_space=pl.ANY)] * 3,
+        fused_kernel,
+        out_shape=jax.ShapeDtypeStruct(tokens.shape, BF),
+        in_specs=[vmem] * 5 + [pl.BlockSpec(memory_space=pl.ANY)] * 3,
         out_specs=vmem,
         scratch_shapes=[
             pltpu.VMEM((2, 256, 4096), BF),
@@ -217,23 +389,34 @@
             pltpu.VMEM((4, 2048, 128), F32),
             pltpu.VMEM((2, 8, 512, 128 * count), BF),
             pltpu.VMEM((64 * count, 8192), BF),
-            pltpu.VMEM((2, rows, 128 * count), F32),
-            pltpu.SemaphoreType.DMA((2, 2)),
+            pltpu.VMEM((2, 256, 128 * count), F32),
+            pltpu.VMEM((8, 256, 1024), BF),
+            pltpu.VMEM((8, 64, 128), F32),
+            pltpu.VMEM((4, 256, 1024), F32),
+            pltpu.VMEM((64, 1024), F32),
+            pltpu.VMEM((4, 256, 1024), BF),
+            pltpu.VMEM((4, 256, 1024), BF),
+            pltpu.VMEM((4, 2, 64, 1024), BF),
+            pltpu.VMEM((4, 2, 64, 1024), BF),
+            pltpu.VMEM((4, 2, 32, 1024), BF),
+            pltpu.VMEM((4, 2, 32, 1024), BF),
+            pltpu.VMEM((4, 64, 1024), BF),
+            pltpu.VMEM((4, 64, 1024), BF),
+            dma((2, 2)),
+            dma((8,)), dma((8,)),
+            dma((4, 2)), dma((4, 2)),
+            dma((4, 2)), dma((4, 2)),
+            dma((4, 2)), dma((4, 2)),
+            dma((4,)), dma((4,)),
+            dma((4,)), dma((4,)),
+            dma((4, 2)), dma((4, 2)),
+            dma((4, 2)), dma((4, 2)),
+            dma((4,)), dma((4,)),
         ],
-        compiler_params=pltpu.CompilerParams(vmem_limit_bytes=60 * 1024 * 1024),
-    )(x, gate_ids, up_ids, down_ids, gate_blocks, up_blocks, down_blocks)
-
-
-def fused(tokens, norm_gain, gate_blocks, gate_ids, up_blocks, up_ids, down_blocks, down_ids):
-    rows, width = tokens.shape
-    values = tokens.astype(F32)
-    total = lax.psum(jnp.sum(values * values, axis=-1, keepdims=True), "wide")
-    normed = (values * lax.rsqrt(total / 8192.0 + 1e-05) * norm_gain.astype(F32)).astype(BF)
-    turned = normed.reshape(rows, width // 64, 32, 2).transpose(0, 3, 2, 1).reshape(rows, width)
-    x = lax.all_gather(turned, ("wide", "narrow"), axis=0, tiled=False).reshape(8, 4 * rows, width)
-    part = compute(x, gate_ids, up_ids, down_ids, gate_blocks, up_blocks, down_blocks)
-    part = part.reshape(32 * rows, width)
-    return lax.psum_scatter(part, ("wide", "narrow"), scatter_dimension=0, tiled=True).astype(BF)
+        compiler_params=pltpu.CompilerParams(
+            vmem_limit_bytes=62 * 1024 * 1024, collective_id=0, has_side_effects=True
+        ),
+    )(tokens, norm_gain.reshape(1, width), gate_ids, up_ids, down_ids, gate_blocks, up_blocks, down_blocks)
 
 
 def solution(mesh):

time: 360 us -> 121 us (0.34)
  waiting for transfers between devices: 243 us -> 0 us
  Pallas kernels: 81.1 us -> 118 us
  blocking collectives: 18.1 us -> 0 us
  between operations: 13.4 us -> 0.01 us
    reduce_scatter x1 -> x0, waiting for transfers between devices: 182 us -> none  [fused(): lax.psum_scatter(part, ('wide', 'narrow'), scatter_dimension=0, tiled=True)]
    all_gather x1 -> x0, waiting for transfers between devices: 60.3 us -> none  [fused(): lax.all_gather(turned, ('wide', 'narrow'), axis=0, tiled=False)]
    pallas_call x1, Pallas kernels: 81.1 us -> 118 us  [fused(): pl.pallas_call(fused_kernel, out_shape=jax.ShapeDtypeStruct(tokens.shape,...]
    psum x1 -> x0, blocking collectives: 18.1 us -> none  [fused(): total = lax.psum(jnp.sum(values * values, axis=-1, keepdims=True), 'wide')]
  transfers between devices with their start and end apart: 2 -> 0, of which waited for: 2 -> 0; matrix products, arithmetic and copies ran while one was open for 0% -> 0% of each run, Pallas kernels for 0% -> 0%
where the time goes in v2:
time: 121 us; the launch traced here: 120 us
  Pallas kernels  118 us (98%)
  local copies, waits for them, and re-layouts  2.85 us (2%)
    pallas_call x1, Pallas kernels, fused(): pl.pallas_call(fused_kernel, out_shape=jax.ShapeDtypeStruct(tokens.shape,...  118 us

profile of v2, /device:TPU:0, one launch (start us, length us, event | category | flops | bytes accessed | tf_op | source)
XLA Modules:
  0.0 120.4 jit_solution(6028537796032386063)
XLA Ops:
  0.0 1.3 %reshape.3.gain = bf16[1,1024]{1,0:T(2,128)(2,1)} reshape(bf16[1024]{0:T(1024)(128)(2,1)} %param.9) | data formatting | bytes 4096 | tf_op jit(solution)/shard_map/reshape | solution.py:419
  1.3 117.5 %shard_map.82 = bf16[64,1024]{1,0:T(8,128)(2,1)} custom-call(bf16[64,1024]{1,0:T(8,128)(2,1)} %tok.1, bf16[1,1024]{1,0:T(2,128)(2,1)} %reshape.3.gain, s32[8,80]{1,0:T(8,128)} %gi.1, s32[8,80]{1,0:T(8,128)} %ui.1, s32[8,80]{1,0:T(8,128)} %di.1, bf16[8,80,4096]{2,1,0:T(8,128)(2,1)} %gb.1, bf16[8,80,4096]{2,1,0:T(8,128)(2,1)} %ub.1, bf16[8,80,4096]{2,1,0:T(8,128)(2,1)} %db.1), custom_call_target="tpu_custom_call" | custom-call | tf_op jit(solution)/shard_map/pallas_call | solution.py:381
  118.8 1.6 %copy.10 = bf16[64,1024]{1,0:T(8,128)(2,1)} copy(bf16[64,1024]{1,0:T(8,128)(2,1)} %shard_map.82) | data formatting | bytes 262144

commit v3 on v2

--- a/solution.py
+++ b/solution.py
@@ -8,6 +8,7 @@
 from jax.sharding import PartitionSpec as P
 
 BLOCK = 64
+STRIDE = 40
 BF = jnp.bfloat16
 F32 = jnp.float32
 
@@ -139,7 +140,7 @@
                     self.in_w[p, :, at, column : column + 128] = v.astype(BF).reshape(8, 16, 128)
             return carry
 
-        lax.fori_loop(0, 16, body, 0)
+        lax.fori_loop(0, 16, body, 0, unroll=16)
 
     def place_down(self, slot, q):
         low = low_half(64)
@@ -150,19 +151,23 @@
                 for e in range(2):
                     a = s[128 * e : 128 * e + 64, 128 * k : 128 * k + 128]
                     b = s[128 * e + 64 : 128 * e + 128, 128 * k : 128 * k + 128]
-                    at = pl.ds(2 * c + k, 64, stride=32)
+                    at = pl.ds(2 * c + k, 64, stride=STRIDE)
                     self.turn[2 * e, at, :] = jnp.where(low, a, swap(b))
                     self.turn[2 * e + 1, at, :] = jnp.where(low, swap(a), b)
             return carry
 
-        lax.fori_loop(0, 16, body, 0)
-        for e in range(2):
-            for p in range(2):
-                first = p * 64 * self.pairs + (2 * q + e) * 32
-                for b in range(64):
-                    self.down_w[first : first + 32, 128 * b : 128 * b + 128] = self.turn[
-                        2 * e + p, 32 * b : 32 * b + 32, :
-                    ].astype(BF)
+        lax.fori_loop(0, 16, body, 0, unroll=16)
+
+        def back(b, carry):
+            for e in range(2):
+                for p in range(2):
+                    first = p * 64 * self.pairs + (2 * q + e) * 32
+                    lanes = pl.ds(pl.multiple_of(128 * b, 128), 128)
+                    at = pl.ds(pl.multiple_of(STRIDE * b, 8), 32)
+                    self.down_w[first : first + 32, lanes] = self.turn[2 * e + p, at, :].astype(BF)
+            return carry
+
+        lax.fori_loop(0, 64, back, 0, unroll=64)
 
 
 def gather_product(x_ref, in_w, acc, w, first):
@@ -289,11 +294,12 @@
         c.start()
     go_first(0)
     after = {
-        1: [(go_first, 1), (go_second, 0), (go_first, 2), (go_first, 3)],
-        2: [(go_second, 1), (go_last, 0)],
-        3: [(go_second, 2), (go_last, 1)],
-        4: [(go_second, 3), (go_last, 2)],
-        5: [(go_last, 3)],
+        3: [(go_first, 1), (go_second, 0)],
+        5: [(go_first, 2), (go_first, 3)],
+        7: [(go_second, 1), (go_last, 0)],
+        8: [(go_second, 2), (go_last, 1)],
+        9: [(go_second, 3), (go_last, 2)],
+        10: [(go_last, 3)],
     }
     for n in range(1, len(panels.steps)):
         panels.step(n)
@@ -386,7 +392,7 @@
         scratch_shapes=[
             pltpu.VMEM((2, 256, 4096), BF),
             pltpu.VMEM((256, 256), BF),
-            pltpu.VMEM((4, 2048, 128), F32),
+            pltpu.VMEM((4, 64 * STRIDE, 128), F32),
             pltpu.VMEM((2, 8, 512, 128 * count), BF),
             pltpu.VMEM((64 * count, 8192), BF),
             pltpu.VMEM((2, 256, 128 * count), F32),

time: 121 us -> 77.1 us (0.64)
  Pallas kernels: 118 us -> 73.9 us
    pallas_call x1, Pallas kernels: 118 us -> 73.9 us  [fused(): pl.pallas_call(fused_kernel, out_shape=jax.ShapeDtypeStruct(tokens.shape,...]
where the time goes in v3:
time: 77.1 us; the launch traced here: 76.8 us
  Pallas kernels  73.9 us (96%)
  local copies, waits for them, and re-layouts  2.85 us (4%)
    pallas_call x1, Pallas kernels, fused(): pl.pallas_call(fused_kernel, out_shape=jax.ShapeDtypeStruct(tokens.shape,...  73.9 us
    unnamed x1, local copies, waits for them, and re-layouts  1.57 us

profile of v3, /device:TPU:0, one launch (start us, length us, event | category | flops | bytes accessed | tf_op | source)
XLA Modules:
  0.0 76.8 jit_solution(12342600736725017937)
XLA Ops:
  0.0 1.3 %reshape.3.gain = bf16[1,1024]{1,0:T(2,128)(2,1)} reshape(bf16[1024]{0:T(1024)(128)(2,1)} %param.9) | data formatting | bytes 4096 | tf_op jit(solution)/shard_map/reshape | solution.py:425
  1.3 73.9 %shard_map.82 = bf16[64,1024]{1,0:T(8,128)(2,1)} custom-call(bf16[64,1024]{1,0:T(8,128)(2,1)} %tok.1, bf16[1,1024]{1,0:T(2,128)(2,1)} %reshape.3.gain, s32[8,80]{1,0:T(8,128)} %gi.1, s32[8,80]{1,0:T(8,128)} %ui.1, s32[8,80]{1,0:T(8,128)} %di.1, bf16[8,80,4096]{2,1,0:T(8,128)(2,1)} %gb.1, bf16[8,80,4096]{2,1,0:T(8,128)(2,1)} %ub.1, bf16[8,80,4096]{2,1,0:T(8,128)(2,1)} %db.1), custom_call_target="tpu_custom_call" | custom-call | tf_op jit(solution)/shard_map/pallas_call | solution.py:387
  75.2 1.6 %copy.10 = bf16[64,1024]{1,0:T(8,128)(2,1)} copy(bf16[64,1024]{1,0:T(8,128)(2,1)} %shard_map.82) | data formatting | bytes 262144

commit v4 on v3

--- a/solution.py
+++ b/solution.py
@@ -329,7 +329,8 @@
     for e in order:
         send0[e] = product(2 * plane(e) + 1 - core).astype(BF)
         hop0[e].start()
-    for e in order:
+
+    def keep(e):
         q[e] = product(2 * plane(e) + core)
 
     def go_hop1(e):
@@ -362,10 +363,13 @@
         if e:
             hop3[e].start()
 
-    for k in range(6):
-        for lag, act in enumerate((go_hop1, go_hop2, go_hop3)):
-            if 0 <= k - lag < 4:
-                act(order[k - lag])
+    reduction = (
+        (keep, 1), (keep, 2), (go_hop1, 1), (keep, 3), (go_hop1, 2), (keep, 0), (go_hop1, 3),
+        (go_hop2, 1), (go_hop1, 0), (go_hop2, 2), (go_hop3, 1), (go_hop2, 3), (go_hop3, 2),
+        (go_hop2, 0), (go_hop3, 3), (go_hop3, 0),
+    )
+    for act, e in reduction:
+        act(e)
     value = own[...]
     for e in (1, 2, 3):
         hop3[e].wait_recv()

time: 77.1 us -> 79.1 us (1.026)
  Pallas kernels: 73.9 us -> 76 us
    pallas_call x1, Pallas kernels: 73.9 us -> 76 us  [fused(): pl.pallas_call(fused_kernel, out_shape=jax.ShapeDtypeStruct(tokens.shape,...]
where the time goes in v4:
time: 79.1 us; the launch traced here: 78.8 us
  Pallas kernels  76 us (96%)
  local copies, waits for them, and re-layouts  2.85 us (4%)
    pallas_call x1, Pallas kernels, fused(): pl.pallas_call(fused_kernel, out_shape=jax.ShapeDtypeStruct(tokens.shape,...  76 us

profile of v4, /device:TPU:0, one launch (start us, length us, event | category | flops | bytes accessed | tf_op | source)
XLA Modules:
  0.0 78.8 jit_solution(6480089209216195549)
XLA Ops:
  0.0 1.3 %reshape.3.gain = bf16[1,1024]{1,0:T(2,128)(2,1)} reshape(bf16[1024]{0:T(1024)(128)(2,1)} %param.9) | data formatting | bytes 4096 | tf_op jit(solution)/shard_map/reshape | solution.py:429
  1.3 76.0 %shard_map.82 = bf16[64,1024]{1,0:T(8,128)(2,1)} custom-call(bf16[64,1024]{1,0:T(8,128)(2,1)} %tok.1, bf16[1,1024]{1,0:T(2,128)(2,1)} %reshape.3.gain, s32[8,80]{1,0:T(8,128)} %gi.1, s32[8,80]{1,0:T(8,128)} %ui.1, s32[8,80]{1,0:T(8,128)} %di.1, bf16[8,80,4096]{2,1,0:T(8,128)(2,1)} %gb.1, bf16[8,80,4096]{2,1,0:T(8,128)(2,1)} %ub.1, bf16[8,80,4096]{2,1,0:T(8,128)(2,1)} %db.1), custom_call_target="tpu_custom_call" | custom-call | tf_op jit(solution)/shard_map/pallas_call | solution.py:391
  77.3 1.6 %copy.10 = bf16[64,1024]{1,0:T(8,128)(2,1)} copy(bf16[64,1024]{1,0:T(8,128)(2,1)} %shard_map.82) | data formatting | bytes 262144
